TPU v7x, 256 devices: a whole 4x4x8 slice. The times are simulated.
256 devices in a mesh: pa: 256 (over z, y, x, core).
Axes of the slice: x: 4, y: 4, z: 8, core: 2. Of those that a mesh axis runs over, the one named last changes fastest.
Arguments:
- coefficients: bfloat16 [196608, 3072], P('pa'), may hold values from -40 to 40, as said below
- masks: int32 [196608, 48], P('pa'), may hold values 0 or 1
Outputs:
- correlation_band: bfloat16 [196608, 3840], P('pa')
Inputs may be any that keep to these rules, and one draw needn't show every extreme that they name: `coefficients`: real parts in the first 1536 columns, imaginary parts in the last 1536.
All inputs are finite; a program needn't handle non-finite values. No bound on the sum of `masks` on one device may be relied on, other than what follows from the above.
Results may differ from a plain program's by a relative error of at most 0.001.
Values may be sent and summed in bfloat16 or wider, within the bound.
A program may use at most 192 MiB of HBM per device.

v0:
```python
import jax
import jax.numpy as jnp
from jax import lax
from jax.sharding import PartitionSpec as P

K = 1536
G = 48


ridge_term = 1.0


def from_behind(value, axis, steps):
    count = lax.axis_size(axis)
    pairs = [(source, (source + steps) % count) for source in range(count)]
    return lax.ppermute(value, axis, pairs)


def prepare(coeff, mask_rows):
    rows = coeff.shape[0]
    mask_float = mask_rows.astype(jnp.float32)
    expanded = (mask_float[:, :, None] * jnp.ones((1, 1, K // G), jnp.float32)).reshape(rows, K)
    expanded = jnp.concatenate([expanded, expanded], axis=1).astype(jnp.bfloat16)
    masked = coeff * expanded
    squared = masked.astype(jnp.float32) ** 2
    power_sum = (squared[:, :K] + squared[:, K:]).reshape(rows, G, K // G).sum(axis=2)
    return (masked, mask_float, power_sum)


def score_tile(first, second):
    numerator = lax.dot_general(
        first[0], second[0], (((1,), (1,)), ((), ())), preferred_element_type=jnp.float32
    )
    norm_left = jnp.dot(first[2], second[1].T, precision=lax.Precision.HIGHEST)
    norm_right = jnp.dot(first[1], second[2].T, precision=lax.Precision.HIGHEST)
    scores = numerator / jnp.sqrt((norm_left + ridge_term) * (norm_right + ridge_term))
    return scores.astype(jnp.bfloat16)


def on_device(coefficients, masks):
    mask_wire = masks.astype(jnp.bfloat16)
    own_parts = prepare(coefficients, mask_wire)
    left_coeff, left_mask = from_behind((coefficients, mask_wire), "pa", 1)
    left_parts = prepare(left_coeff, left_mask)
    centre_tile = score_tile(own_parts, own_parts)
    lower_tile = score_tile(own_parts, left_parts)
    second_coeff, second_mask = from_behind((left_coeff, left_mask), "pa", 1)
    lower_far = score_tile(own_parts, prepare(second_coeff, second_mask))
    upper_tile = from_behind(lower_tile.T, "pa", -1)
    upper_far = from_behind(lower_far.T, "pa", -2)
    return jnp.concatenate([lower_far, lower_tile, centre_tile, upper_tile, upper_far], axis=1)


def solution(mesh):
    in_specs = (P("pa", None), P("pa", None))
    out_specs = P("pa", None)
    return jax.shard_map(
        on_device, mesh=mesh, in_specs=in_specs, out_specs=out_specs, check_vma=False
    )
```

profile of v0, /device:TPU:0, one launch (start us, length us, event | category | flops | bytes accessed | tf_op | source)
XLA Modules:
  0.0 218.1 jit_solution(15562962687338312360)
XLA Ops:
  0.0 6.6 %copy.28 = bf16[768,3072]{0,1:T(8,128)(2,1)} copy(bf16[768,3072]{1,0:T(8,128)(2,1)} %param.2) | data formatting | bytes 9437184 | tf_op args[0]
  6.6 0.0 collective-permute-start
  6.7 0.0 copy-done.8
  6.7 0.1 collective-permute-start.2
  6.8 0.2 broadcast.15
  6.9 0.0 copy-start.2
  6.9 3.9 %convert_multiply_fusion.2 = f32[768,3072]{0,1:T(8,128)S(1)} fusion(bf16[768,3072]{0,1:T(8,128)(2,1)} %copy.28, bf16[768,1536]{0,1:T(8,128)(2,1)S(1)} %bitcast.63), kind=kLoop, calls=%fused_computation.2 | loop fusion | flops 16515072 | bytes 16515072 | tf_op jit(solution)/shard_map/integer_pow | solution.py:25
  10.8 0.0 copy-done.2
  10.8 2.7 %slice_add_fusion.2 = f32[768,1536]{0,1:T(8,128)} fusion(f32[768,3072]{0,1:T(8,128)S(1)} %convert_multiply_fusion.2), kind=kLoop, calls=%fused_computation.5 | loop fusion | flops 1179648 | bytes 14155776 | tf_op jit(solution)/shard_map/add | solution.py:26
  13.5 2.9 %reduce_sum.27 = f32[768,48]{0,1:T(8,128)S(1)} reduce(f32[768,48,32]{0,2,1:T(8,128)} %bitcast.61, f32[]{:T(128)} %constant.0.clone.1), dimensions={2}, to_apply=%region_0.0 | reduce | flops 1142784 | bytes 4866052 | tf_op jit(solution)/shard_map/reduce_sum | solution.py:26
  16.5 50.5 %collective-permute-done = bf16[768,3072]{0,1:T(8,128)(2,1)} collective-permute-done((bf16[768,3072]{0,1:T(8,128)(2,1)}, bf16[768,3072]{0,1:T(8,128)(2,1)}, u32[]{:S(2)}, u32[]{:S(2)}) %collective-permute-start) | collective-permute-done | bytes 4718624 | tf_op jit(solution)/shard_map/ppermute | solution.py:16
  67.0 0.0 collective-permute-start.1
  67.0 1.1 convolution_add_fusion
  68.1 2.1 copy.36
  70.3 0.0 collective-permute-done.2
  70.3 0.0 collective-permute-start.3
  70.3 2.6 %fusion.20 = f32[768,768]{0,1:T(8,128)} fusion(f32[768,48]{0,1:T(8,128)S(1)} %reduce_sum.27, bf16[768,48]{0,1:T(8,128)(2,1)S(1)} %collective-permute-done.2), kind=kOutput, calls=%fused_computation.40 | convolution fusion | flops 339738624 | bytes 2580480 | tf_op jit(solution)/shard_map/dot_general | solution.py:34
  72.9 54.1 %collective-permute-done.3 = bf16[768,48]{0,1:T(8,128)(2,1)S(1)} collective-permute-done((bf16[768,48]{0,1:T(8,128)(2,1)S(1)}, bf16[768,48]{0,1:T(8,128)(2,1)S(1)}, u32[]{:S(2)}, u32[]{:S(2)}) %collective-permute-start.3) | collective-permute-done | bytes 73760 | tf_op jit(solution)/shard_map/ppermute | solution.py:16
  127.0 1.1 fusion.19
  128.1 1.6 broadcast.17
  129.7 4.5 %convert_multiply_fusion = f32[768,3072]{0,1:T(8,128)S(1)} fusion(bf16[768,3072]{0,1:T(8,128)(2,1)} %collective-permute-done, bf16[768,1536]{0,1:T(8,128)(2,1)} %bitcast.69), kind=kLoop, calls=%fused_computation | loop fusion | flops 16515072 | bytes 16515072 | tf_op jit(solution)/shard_map/integer_pow | solution.py:25
  134.2 2.8 %slice_add_fusion = f32[768,1536]{0,1:T(8,128)} fusion(f32[768,3072]{0,1:T(8,128)S(1)} %convert_multiply_fusion), kind=kLoop, calls=%fused_computation.3 | loop fusion | flops 1179648 | bytes 14155776 | tf_op jit(solution)/shard_map/add | solution.py:26
  137.0 2.9 %reduce_sum.29 = f32[768,48]{0,1:T(8,128)S(1)} reduce(f32[768,48,32]{0,2,1:T(8,128)} %bitcast.62, f32[]{:T(128)} %constant.0.clone.1), dimensions={2}, to_apply=%region_2.0 | reduce | flops 1142784 | bytes 4866052 | tf_op jit(solution)/shard_map/reduce_sum | solution.py:26
  140.0 1.1 fusion.21
  141.1 12.9 %fusion.10 = (bf16[768,768]{0,1:T(8,128)(2,1)}, f32[768,768]{0,1:T(8,128)S(1)}) fusion(f32[768,768]{1,0:T(8,128)S(1)} %fusion.21, f32[768,768]{0,1:T(8,128)} %fusion.20, bf16[768,3072]{0,1:T(8,128)(2,1)} %collective-permute-done, bf16[768,1536]{0,1:T(8,128)(2,1)} %bitcast.70, bf16[768,3072]{0,1:T(8,128)(2,1)} %copy.28, bf16[768,1536]{0,1:T(8,128)(2,1)} %bitcast.64), kind=kOutput, calls=%fused_computation.24 | convolution fusion | flops 3655139328 | bytes 22413312 | tf_op jit(solution)/shard_map/dot_general | solution.py:31
  154.0 1.6 fusion.4
  155.6 0.0 collective-permute-start.4
  155.6 0.0 collective-permute-done.1
  155.6 1.6 broadcast.16
  157.1 4.3 %convert_multiply_fusion.1 = f32[768,3072]{0,1:T(8,128)S(1)} fusion(bf16[768,3072]{0,1:T(8,128)(2,1)} %collective-permute-done.1, bf16[768,1536]{0,1:T(8,128)(2,1)} %bitcast.67), kind=kLoop, calls=%fused_computation.1 | loop fusion | flops 16515072 | bytes 16515072 | tf_op jit(solution)/shard_map/integer_pow | solution.py:25
  161.5 2.8 %slice_add_fusion.1 = f32[768,1536]{0,1:T(8,128)} fusion(f32[768,3072]{0,1:T(8,128)S(1)} %convert_multiply_fusion.1), kind=kLoop, calls=%fused_computation.4 | loop fusion | flops 1179648 | bytes 14155776 | tf_op jit(solution)/shard_map/add | solution.py:26
  164.2 2.9 %reduce_sum.28 = f32[768,48]{0,1:T(8,128)S(1)} reduce(f32[768,48,32]{0,2,1:T(8,128)} %bitcast.60, f32[]{:T(128)} %constant.0.clone.1), dimensions={2}, to_apply=%region_1.0 | reduce | flops 1142784 | bytes 4866052 | tf_op jit(solution)/shard_map/reduce_sum | solution.py:26
  167.2 3.5 %fusion = (f32[768,768]{0,1:T(8,128)}, f32[768,768]{0,1:T(8,128)}) fusion(f32[768,768]{1,0:T(8,128)S(1)} %fusion.19, f32[768,48]{0,1:T(8,128)S(1)} %reduce_sum.28, bf16[768,48]{0,1:T(8,128)(2,1)S(1)} %convert.18), kind=kOutput, calls=%fused_computation.10 | convolution fusion | flops 341508096 | bytes 7299072 | tf_op jit(solution)/shard_map/dot_general | solution.py:35
  170.7 3.1 %copy.37 = f32[768,768]{1,0:T(8,128)} copy(f32[768,768]{0,1:T(8,128)} %get-tuple-element.7) | data formatting | bytes 4718592 | tf_op jit(solution)/shard_map/sqrt | solution.py:36
  173.8 13.3 %fusion.1 = (bf16[768,768]{1,0:T(8,128)(2,1)}, f32[768,768]{0,1:T(8,128)}) fusion(f32[768,768]{1,0:T(8,128)} %copy.37, bf16[768,3072]{0,1:T(8,128)(2,1)} %collective-permute-done.1, bf16[768,1536]{0,1:T(8,128)(2,1)} %bitcast.68, bf16[768,3072]{0,1:T(8,128)(2,1)} %copy.28, bf16[768,1536]{0,1:T(8,128)(2,1)} %bitcast.65), kind=kOutput, calls=%fused_computation.12 | convolution fusion | flops 3653369856 | bytes 20054016 | tf_op jit(solution)/shard_map/dot_general | solution.py:31
  187.1 0.0 collective-permute-start.5
  187.1 9.6 %fusion.7 = bf16[768,768]{0,1:T(8,128)(2,1)} fusion(f32[768,768]{0,1:T(8,128)S(1)} %copy-done.1, f32[768,768]{1,0:T(8,128)S(1)} %copy-done.6, bf16[768,3072]{0,1:T(8,128)(2,1)} %copy.28, bf16[768,1536]{0,1:T(8,128)(2,1)S(1)} %bitcast.66), kind=kOutput, calls=%fused_computation.20 | convolution fusion | flops 3639803904 | bytes 12976128 | tf_op jit(solution)/shard_map/dot_general | solution.py:31
  196.7 1.6 copy.39
  198.2 2.4 %copy.38 = bf16[768,768]{1,0:T(8,128)(2,1)} copy(bf16[768,768]{0,1:T(8,128)(2,1)} %get-tuple-element.5) | data formatting | bytes 2359296 | tf_op jit(solution)/shard_map/convert_element_type | solution.py:37
  200.7 3.0 %copy.33 = f32[768,768]{1,0:T(8,128)} copy(f32[768,768]{0,1:T(8,128)} %get-tuple-element.10) | data formatting | bytes 4718592 | tf_op jit(solution)/shard_map/dot_general | solution.py:31
  203.7 2.9 %fusion.16 = bf16[768,3840]{1,0:T(8,128)(2,1)S(1)} fusion(f32[768,768]{1,0:T(8,128)} %copy.33, f32[768,768]{0,1:T(8,128)} %get-tuple-element.8, f32[768,768]{1,0:T(8,128)S(1)} %fusion.19), kind=kLoop, calls=%fused_computation.32 | loop fusion | flops 2949119 | bytes 8257536
  206.7 0.1 constant_dynamic-update-slice_fusion.3
  206.8 0.1 constant_dynamic-update-slice_fusion.2
  206.8 0.0 collective-permute-done.4
  206.9 1.3 constant_dynamic-update-slice_fusion.1
  208.2 0.0 copy-start.7
  208.2 7.5 %collective-permute-done.5 = bf16[768,768]{1,0:T(8,128)(2,1)} collective-permute-done((bf16[768,768]{1,0:T(8,128)(2,1)}, bf16[768,768]{1,0:T(8,128)(2,1)}, u32[]{:S(2)}, u32[]{:S(2)}) %collective-permute-start.5) | collective-permute-done | bytes 1179680 | tf_op jit(solution)/shard_map/ppermute | solution.py:16
  215.8 2.4 %constant_dynamic-update-slice_fusion = bf16[768,3840]{1,0:T(8,128)(2,1)} fusion(bf16[768,3840]{1,0:T(8,128)(2,1)} %copy-done.7, bf16[768,768]{1,0:T(8,128)(2,1)} %collective-permute-done.5), kind=kLoop, calls=%fused_computation.33 | loop fusion | bytes 2359296 | tf_op jit(solution)/shard_map/concatenate | solution.py:51
  (15 shorter events, 0.0 us)
Async XLA Ops:
  0.0 6.7 %copy-start.8 = (s32[768,48]{0,1:T(8,128)S(1)}, s32[768,48]{0,1:T(8,128)}, u32[]{:S(2)}) copy-start(s32[768,48]{0,1:T(8,128)} %param.3) | copy-start | bytes 442372
  6.6 60.3 %collective-permute-start = (bf16[768,3072]{0,1:T(8,128)(2,1)}, bf16[768,3072]{0,1:T(8,128)(2,1)}, u32[]{:S(2)}, u32[]{:S(2)}) collective-permute-start(bf16[768,3072]{0,1:T(8,128)(2,1)} %copy.28), channel_id=1, source_target_pairs={{0,1},{1,2},{2,3},{3,4},{4,5},{5,6},{6,7},{7,8},{8,9},{9,10},{10,1... | collective-permute-start | bytes 14155784 | tf_op jit(solution)/shard_map/ppermute | solution.py:16
  6.7 63.6 %collective-permute-start.2 = (bf16[768,48]{0,1:T(8,128)(2,1)S(1)}, bf16[768,48]{0,1:T(8,128)(2,1)S(1)}, u32[]{:S(2)}, u32[]{:S(2)}) collective-permute-start(bf16[768,48]{0,1:T(8,128)(2,1)S(1)} %convert.18), channel_id=1, source_target_pairs={{0,1},{1,2},{2,3},{3,4},{4,5},{5,6},{6,7},{7,8},{8,9},{9,10},{10,1... | collective-permute-start | bytes 221192 | tf_op jit(solution)/shard_map/ppermute | solution.py:16
  6.9 3.9 %copy-start.2 = (bf16[768,48,32]{0,2,1:T(8,128)(2,1)}, bf16[768,48,32]{0,2,1:T(8,128)(2,1)S(1)}, u32[]{:S(2)}) copy-start(bf16[768,48,32]{0,2,1:T(8,128)(2,1)S(1)} %broadcast.15) | copy-start | bytes 7077892
  67.0 88.6 %collective-permute-start.1 = (bf16[768,3072]{0,1:T(8,128)(2,1)}, bf16[768,3072]{0,1:T(8,128)(2,1)}, u32[]{:S(2)}, u32[]{:S(2)}) collective-permute-start(bf16[768,3072]{0,1:T(8,128)(2,1)} %collective-permute-done), channel_id=1, source_target_pairs={{0,1},{1,2},{2,3},{3,4},{4,5},{5,6},{6,7},{7,8},{8,9},{9,10},{10,1... | collective-permute-start | bytes 14155784 | tf_op jit(solution)/shard_map/ppermute | solution.py:16
  68.1 4.8 %copy-start = (f32[768,768]{0,1:T(8,128)}, f32[768,768]{0,1:T(8,128)S(1)}, u32[]{:S(2)}) copy-start(f32[768,768]{0,1:T(8,128)S(1)} %convolution_add_fusion) | copy-start | bytes 7077892
  70.3 56.7 %collective-permute-start.3 = (bf16[768,48]{0,1:T(8,128)(2,1)S(1)}, bf16[768,48]{0,1:T(8,128)(2,1)S(1)}, u32[]{:S(2)}, u32[]{:S(2)}) collective-permute-start(bf16[768,48]{0,1:T(8,128)(2,1)S(1)} %collective-permute-done.2), channel_id=1, source_target_pairs={{0,1},{1,2},{2,3},{3,4},{4,5},{5,6},{6,7},{7,8},{8,9},{9,10},{10,1... | collective-permute-start | bytes 221192 | tf_op jit(solution)/shard_map/ppermute | solution.py:16
  141.1 12.9 %copy-start.4 = (f32[768,768]{0,1:T(8,128)S(1)}, f32[768,768]{0,1:T(8,128)}, u32[]{:S(2)}) copy-start(f32[768,768]{0,1:T(8,128)} %fusion.20) | copy-start | bytes 7077892
  155.6 51.3 %collective-permute-start.4 = (bf16[768,768]{1,0:T(8,128)(2,1)}, bf16[768,768]{1,0:T(8,128)(2,1)}, u32[]{:S(2)}, u32[]{:S(2)}) collective-permute-start(bf16[768,768]{1,0:T(8,128)(2,1)} %fusion.4), channel_id=1, source_target_pairs={{0,255},{1,0},{2,1},{3,2},{4,3},{5,4},{6,5},{7,6},{8,7},{9,8},{10,... | collective-permute-start | bytes 3538952 | tf_op jit(solution)/shard_map/ppermute | solution.py:16
  173.8 13.3 %copy-start.1 = (f32[768,768]{0,1:T(8,128)S(1)}, f32[768,768]{0,1:T(8,128)}, u32[]{:S(2)}) copy-start(f32[768,768]{0,1:T(8,128)} %copy-done) | copy-start | bytes 7077892
  173.8 13.3 %copy-start.3 = (bf16[768,48,32]{0,2,1:T(8,128)(2,1)S(1)}, bf16[768,48,32]{0,2,1:T(8,128)(2,1)}, u32[]{:S(2)}) copy-start(bf16[768,48,32]{0,2,1:T(8,128)(2,1)} %copy-done.2) | copy-start | bytes 7077892
  173.8 13.3 %copy-start.6 = (f32[768,768]{1,0:T(8,128)S(1)}, f32[768,768]{1,0:T(8,128)}, u32[]{:S(2)}) copy-start(f32[768,768]{1,0:T(8,128)} %copy.36) | copy-start | bytes 7077892
  187.1 28.7 %collective-permute-start.5 = (bf16[768,768]{1,0:T(8,128)(2,1)}, bf16[768,768]{1,0:T(8,128)(2,1)}, u32[]{:S(2)}, u32[]{:S(2)}) collective-permute-start(bf16[768,768]{1,0:T(8,128)(2,1)} %get-tuple-element.9), channel_id=1, source_target_pairs={{0,254},{1,255},{2,0},{3,1},{4,2},{5,3},{6,4},{7,5},{8,6},{9,7},{1... | collective-permute-start | bytes 3538952 | tf_op jit(solution)/shard_map/ppermute | solution.py:16
  203.7 2.9 %copy-start.5 = (bf16[768,768]{1,0:T(8,128)(2,1)S(1)}, bf16[768,768]{1,0:T(8,128)(2,1)}, u32[]{:S(2)}) copy-start(bf16[768,768]{1,0:T(8,128)(2,1)} %copy.38) | copy-start | bytes 3538948
  208.2 7.6 %copy-start.7 = (bf16[768,3840]{1,0:T(8,128)(2,1)}, bf16[768,3840]{1,0:T(8,128)(2,1)S(1)}, u32[]{:S(2)}) copy-start(bf16[768,3840]{1,0:T(8,128)(2,1)S(1)} %constant_dynamic-update-slice_fusion.1) | copy-start | bytes 17694724
where the time goes:
time: 221 us; the launch traced here: 218 us
  waiting for transfers between devices  112 us (51%)
  matrix products  45.2 us (20%)
  other arithmetic  34.3 us (16%)
  local copies, waits for them, and re-layouts  26.2 us (12%)
    ppermute x6, waiting for transfers between devices, from_behind(): return lax.ppermute(value, axis, pairs)  112 us
    dot_general x3, matrix products, score_tile(): lax.dot_general(first[0], second[0], (((1,), (1,)), ((), ())), preferred_...  35.7 us
    integer_pow x3, other arithmetic, prepare(): squared = masked.astype(jnp.float32) ** 2  12.7 us
    reduce_sum x3, other arithmetic, prepare(): (squared[:, :K] + squared[:, K:]).reshape(rows, G, K // G).sum(axis=2)  8.79 us
    add x3, other arithmetic, prepare(): squared[:, :K] + squared[:, K:]  8.3 us
    unnamed x22, local copies, waits for them, and re-layouts  8.19 us
    dot_general x3, matrix products, score_tile(): norm_left = jnp.dot(first[2], second[1].T, precision=lax.Precision.HIGHEST)  4.86 us
    dot_general x2, matrix products, score_tile(): norm_right = jnp.dot(first[1], second[2].T, precision=lax.Precision.HIGHEST)  4.64 us
  transfers between devices with their start and end apart: 6, of which 3 were waited for; matrix products, arithmetic and copies ran while one was open for 44% of the time, Pallas kernels for 0%

commit v1 on v0

v1 whole, which is shorter than its diff:
```python
import functools

import jax
import jax.numpy as jnp
from jax import lax
from jax.experimental import pallas as pl
from jax.experimental.pallas import tpu as pltpu
from jax.sharding import PartitionSpec as P

K = 1536
G = 48
R = 768
BF = jnp.bfloat16
F32 = jnp.float32
MESH = pl.DeviceIdType.MESH

ridge_term = 1.0

CH = 128
NCH = R // CH
LW = 256
ROWS = 256
KP = 256


def nt(x, y):
    return lax.dot_general(x, y, (((1,), (1,)), ((), ())), preferred_element_type=F32)


def nn(x, y):
    return jnp.dot(x, y, preferred_element_type=F32)


def tn(x, y):
    return lax.dot_general(x, y, (((0,), (0,)), ((), ())), preferred_element_type=F32)


def iota(shape, dim):
    return lax.broadcasted_iota(jnp.int32, shape, dim)


def remote(src, dst, send_sem, recv_sem, device):
    return pltpu.make_async_remote_copy(
        src_ref=src, dst_ref=dst, send_sem=send_sem, recv_sem=recv_sem,
        device_id=(device,), device_id_type=MESH,
    )


def rows_of(c):
    return pl.ds(pl.multiple_of(c * CH, CH), CH)


def kernel(n, coeff, masks, out, a, s, e, pa, ma, ps, ms, pe, me, mt, mte, far, fart,
           expand, rep, mask_in, load_sem, mask_sem,
           eb_send, eb_recv, em_send, em_recv, sb_send, sb_recv, sp_send, sp_recv,
           fe_send, fe_recv, fs_send, fs_recv):
    d = lax.axis_index("pa")
    odd = lax.rem(d, 2)
    sib = d + 1 - 2 * odd
    ext = lax.rem(d + n + 2 * odd - 1, n)
    band_s = (3 - 2 * odd) * R
    band_e = (1 + 2 * odd) * R
    band_far_e = 4 * odd * R
    band_far_s = (4 - 4 * odd) * R
    band_sib_far = 4 * odd * R
    band_ext_far = (4 - 4 * odd) * R

    def cols(band, c):
        return pl.ds(pl.multiple_of(band + c * CH, CH), CH)

    def whole(band):
        return pl.ds(pl.multiple_of(band, R), R)

    load_mask = pltpu.make_async_copy(masks, mask_in, mask_sem)
    load_mask.start()

    def load(c):
        return pltpu.make_async_copy(coeff.at[rows_of(c), :], a.at[rows_of(c), :], load_sem.at[c])

    def block_to_ext(c):
        return remote(coeff.at[rows_of(c), :], e.at[rows_of(c), :], eb_send.at[c], eb_recv.at[c], ext)

    def block_to_sib(c):
        return remote(a.at[rows_of(c), :], s.at[rows_of(c), :], sb_send.at[c], sb_recv.at[c], sib)

    def far_to_ext(c):
        return remote(fart.at[rows_of(c), :], out.at[rows_of(c), whole(band_ext_far)],
                      fe_send.at[c], fe_recv.at[c], ext)

    def far_to_sib(c):
        return remote(far.at[:, cols(0, c)], out.at[:, cols(band_sib_far, c)],
                      fs_send.at[c], fs_recv.at[c], sib)

    mask_to_ext = remote(mt, mte, em_send, em_recv, ext)
    m_to_sib = remote(ma, ms, sp_send.at[0], sp_recv.at[0], sib)
    p_to_sib = remote(pa, ps, sp_send.at[1], sp_recv.at[1], sib)

    barrier = pltpu.get_barrier_semaphore()
    pl.semaphore_signal(barrier, inc=1, device_id=(sib,), device_id_type=MESH)
    pl.semaphore_signal(barrier, inc=1, device_id=(ext,), device_id_type=MESH)
    pl.loop(0, NCH)(lambda c: load(c).start())
    pl.semaphore_wait(barrier, 2)

    block_to_ext(0).start()

    load_mask.wait()
    mt[...] = mask_in[...].astype(F32).astype(BF)
    mask_to_ext.start()
    pl.loop(1, NCH)(lambda c: block_to_ext(c).start())
    rep[...] = jnp.where(
        (lax.rem(iota((G, LW), 1), G) == iota((G, LW), 0)) & (iota((G, LW), 1) < 3 * G), 1.0, 0.0
    ).astype(BF)
    ma[...] = tn(mt[...], rep[...]).astype(BF)
    m_to_sib.start()
    expand[...] = jnp.where(
        iota((LW, K), 1) // (K // G) == iota((LW, K), 0), 1.0, 0.0
    ).astype(BF)

    lane = iota((CH, LW), 1)

    def split(x):
        first = x.astype(BF)
        rest = x - first.astype(F32)
        second = rest.astype(BF)
        return first, second, (rest - second.astype(F32)).astype(BF)

    def prepare(c, block, m, p):
        rows = rows_of(c)
        m_rows = m[rows, :]
        power = jnp.zeros((CH, LW), F32)
        for k in range(0, K, KP):
            keep = nn(m_rows, expand[:, k:k + KP]).astype(BF)
            re = block[rows, k:k + KP] * keep
            im = block[rows, K + k:K + k + KP] * keep
            block[rows, k:k + KP] = re
            block[rows, K + k:K + k + KP] = im
            re = re.astype(F32)
            im = im.astype(F32)
            group = jnp.where(
                (lax.rem(iota((KP, LW), 1), G) == (iota((KP, LW), 0) + k) // (K // G))
                & (iota((KP, LW), 1) < 3 * G), 1.0, 0.0
            ).astype(BF)
            for part in split(re * re + im * im):
                power += nn(part, group)
        first, second, third = split(power)
        p[rows, :] = jnp.where(lane < G, first, jnp.where(lane < 2 * G, second, third))

    def score(x, px, mx, i, y, py, my, c):
        left = pl.ds(i, ROWS)
        right = rows_of(c)
        numerator = nt(x[left, :], y[right, :])
        norm_left = nt(px[left, :], my[right, :])
        norm_right = nt(mx[left, :], py[right, :])
        return numerator * lax.rsqrt((norm_left + ridge_term) * (norm_right + ridge_term))

    def near(c, y, py, my, band):
        for i in range(0, R, ROWS):
            out[i:i + ROWS, cols(band, c)] = score(a, pa, ma, i, y, py, my, c).astype(BF)

    @pl.loop(0, NCH)
    def _(c):
        load(c).wait()
        prepare(c, a, ma, pa)
        block_to_sib(c).start()

    p_to_sib.start()

    @pl.loop(0, NCH)
    def _(c):
        near(c, a, pa, ma, 2 * R)

    m_to_sib.wait_recv()
    p_to_sib.wait_recv()

    @pl.loop(0, NCH)
    def _(c):
        block_to_sib(c).wait_recv()
        near(c, s, ps, ms, band_s)

    mask_to_ext.wait_recv()
    me[...] = tn(mte[...], rep[...]).astype(BF)

    @pl.loop(0, NCH)
    def _(c):
        block_to_ext(c).wait_recv()
        prepare(c, e, me, pe)
        for i in range(0, R, ROWS):
            tile = score(s, ps, ms, i, e, pe, me, c)
            fart[rows_of(c), i:i + ROWS] = tile.T.astype(BF)
            far[i:i + ROWS, cols(0, c)] = tile.astype(BF)
        far_to_ext(c).start()
        far_to_sib(c).start()
        near(c, e, pe, me, band_e)

    mask_to_ext.wait_send()
    m_to_sib.wait_send()
    p_to_sib.wait_send()

    @pl.loop(0, NCH)
    def _(c):
        block_to_ext(c).wait_send()
        block_to_sib(c).wait_send()
        far_to_sib(c).wait()
        far_to_ext(c).wait()


def on_device(coefficients, masks):
    n = lax.axis_size("pa")
    block = pltpu.VMEM((R, 2 * K), BF)
    norm = pltpu.VMEM((R, LW), BF)
    dma = pltpu.SemaphoreType.DMA
    return pl.pallas_call(
        functools.partial(kernel, n),
        out_shape=pltpu.VMEM((R, 5 * R), BF),
        in_specs=[pl.BlockSpec(memory_space=pltpu.HBM)] * 2,
        out_specs=pl.BlockSpec(memory_space=pltpu.VMEM),
        scratch_shapes=[
            block, block, block, norm, norm, norm, norm, norm, norm,
            pltpu.VMEM((G, R), BF), pltpu.VMEM((G, R), BF),
            pltpu.VMEM((R, R), BF), pltpu.VMEM((R, R), BF),
            pltpu.VMEM((LW, K), BF), pltpu.VMEM((G, LW), BF),
            pltpu.VMEM((G, R), jnp.int32),
            dma((NCH,)), dma,
            dma((NCH,)), dma((NCH,)), dma, dma, dma((NCH,)), dma((NCH,)), dma((2,)), dma((2,)),
            dma((NCH,)), dma((NCH,)), dma((NCH,)), dma((NCH,)),
        ],
        compiler_params=pltpu.CompilerParams(
            collective_id=0, has_side_effects=True, vmem_limit_bytes=56 * 1024 * 1024
        ),
        cost_estimate=pl.CostEstimate(
            flops=2 * 4 * R * R * 2 * K, bytes_accessed=4 * R * 2 * K, transcendentals=4 * R * R
        ),
        name="band",
    )(coefficients, masks.T)


def solution(mesh):
    return jax.shard_map(
        on_device, mesh=mesh, in_specs=(P("pa", None), P("pa", None)),
        out_specs=P("pa", None), check_vma=False,
    )
```

time: 221 us -> 77.5 us (0.35); the launches traced: 218 us -> 77.5 us
  waiting for transfers between devices: 112 us -> 0 us
  Pallas kernels: 0 us -> 74.9 us
  matrix products: 45.2 us -> 0 us
  other arithmetic: 34.3 us -> 0 us
  local copies, waits for them, and re-layouts: 26.2 us -> 2.58 us
    ppermute x6 -> x0, waiting for transfers between devices: 112 us -> none  [from_behind(): return lax.ppermute(value, axis, pairs)]
    pallas_call x0 -> x1, Pallas kernels: none -> 74.9 us  [on_device(): pl.pallas_call(functools.partial(kernel, n), out_shape=pltpu.VMEM((R, 5 *...]
    dot_general x8 -> x0, matrix products: 45.2 us -> none  [the longest x3 35.7 us: score_tile(): lax.dot_general(first[0], second[0], (((1,), (1,)), ((), ())), preferred_...]
    integer_pow x3 -> x0, other arithmetic: 12.7 us -> none  [prepare(): squared = masked.astype(jnp.float32) ** 2]
    reduce_sum x3 -> x0, other arithmetic: 8.79 us -> none  [prepare(): (squared[:, :K] + squared[:, K:]).reshape(rows, G, K // G).sum(axis=2)]
    add x3 -> x0, other arithmetic: 8.3 us -> none  [prepare(): squared[:, :K] + squared[:, K:]]
    unnamed x22 -> x1, local copies, waits for them, and re-layouts: 8.19 us -> 2.58 us
    convert_element_type x2 -> x0, local copies, waits for them, and re-layouts: 4.01 us -> none  [score_tile(): return scores.astype(jnp.bfloat16)]
  transfers between devices with their start and end apart: 6 -> 0, of which waited for: 3 -> 0; matrix products, arithmetic and copies ran while one was open for 44% -> 0% of each run, Pallas kernels for 0% -> 0%
where the time goes in v1:
time: 77.5 us
  Pallas kernels  74.9 us (97%)
  local copies, waits for them, and re-layouts  2.58 us (3%)
    pallas_call x1, Pallas kernels, on_device(): pl.pallas_call(functools.partial(kernel, n), out_shape=pltpu.VMEM((R, 5 *...  74.9 us
    unnamed x1, local copies, waits for them, and re-layouts  2.58 us

profile of v1, /device:TPU:0, one launch (start us, length us, event | category | flops | bytes accessed | tf_op | source)
XLA Modules:
  0.0 77.5 jit_solution(1999354416906078808)
XLA Ops:
  0.0 74.9 %band.1 = bf16[768,3840]{1,0:T(8,128)(2,1)S(1)} custom-call(bf16[768,3072]{1,0:T(8,128)(2,1)} %coeff.1, s32[48,768]{1,0:T(8,128)} %bitcast.1), custom_call_target="tpu_custom_call" | custom-call | flops 14495514624 | bytes 9437184 | tf_op jit(solution)/shard_map/band/pallas_call | solution.py:212
  74.9 2.6 %copy.4 = bf16[768,3840]{1,0:T(8,128)(2,1)} copy(bf16[768,3840]{1,0:T(8,128)(2,1)S(1)} %band.1) | data formatting | bytes 11796480

commit v2 on v1

--- a/solution.py
+++ b/solution.py
@@ -180,25 +180,38 @@
     mask_to_ext.wait_recv()
     me[...] = tn(mte[...], rep[...]).astype(BF)
 
-    @pl.loop(0, NCH)
-    def _(c):
-        block_to_ext(c).wait_recv()
+    def far_tile(c):
         prepare(c, e, me, pe)
         for i in range(0, R, ROWS):
             tile = score(s, ps, ms, i, e, pe, me, c)
             fart[rows_of(c), i:i + ROWS] = tile.T.astype(BF)
             far[i:i + ROWS, cols(0, c)] = tile.astype(BF)
-        far_to_ext(c).start()
+
+    @pl.loop(0, NCH)
+    def _(c):
+        @pl.when(c == NCH - 1)
+        def _():
+            far_to_ext(0).start()
+            block_to_ext(NCH - 1).wait_send()
+            pl.loop(1, NCH - 1)(lambda j: far_to_ext(j).start())
+
+        block_to_ext(c).wait_recv()
+        far_tile(c)
+
+        @pl.when(c == NCH - 1)
+        def _():
+            far_to_ext(c).start()
+
         far_to_sib(c).start()
         near(c, e, pe, me, band_e)
 
     mask_to_ext.wait_send()
     m_to_sib.wait_send()
     p_to_sib.wait_send()
-
-    @pl.loop(0, NCH)
-    def _(c):
-        block_to_ext(c).wait_send()
+    pl.loop(0, NCH - 1)(lambda c: block_to_ext(c).wait_send())
+
+    @pl.loop(0, NCH)
+    def _(c):
         block_to_sib(c).wait_send()
         far_to_sib(c).wait()
         far_to_ext(c).wait()

time: 77.5 us -> 81.2 us (1.048)
  Pallas kernels: 74.9 us -> 78.5 us
    pallas_call x1, Pallas kernels: 74.9 us -> 78.5 us  [on_device(): pl.pallas_call(functools.partial(kernel, n), out_shape=pltpu.VMEM((R, 5 *...]
where the time goes in v2:
time: 81.2 us; the launch traced here: 81.1 us
  Pallas kernels  78.5 us (97%)
  local copies, waits for them, and re-layouts  2.58 us (3%)
    pallas_call x1, Pallas kernels, on_device(): pl.pallas_call(functools.partial(kernel, n), out_shape=pltpu.VMEM((R, 5 *...  78.5 us
    unnamed x1, local copies, waits for them, and re-layouts  2.58 us

profile of v2, /device:TPU:0, one launch (start us, length us, event | category | flops | bytes accessed | tf_op | source)
XLA Modules:
  0.0 81.1 jit_solution(10336342187267698556)
XLA Ops:
  0.0 78.5 %band.1 = bf16[768,3840]{1,0:T(8,128)(2,1)S(1)} custom-call(bf16[768,3072]{1,0:T(8,128)(2,1)} %coeff.1, s32[48,768]{1,0:T(8,128)} %bitcast.1), custom_call_target="tpu_custom_call" | custom-call | flops 14495514624 | bytes 9437184 | tf_op jit(solution)/shard_map/band/pallas_call | solution.py:225
  78.5 2.6 %copy.4 = bf16[768,3840]{1,0:T(8,128)(2,1)} copy(bf16[768,3840]{1,0:T(8,128)(2,1)S(1)} %band.1) | data formatting | bytes 11796480

commit v3 on v1

v3 whole, which is shorter than its diff:
```python
import functools

import jax
import jax.numpy as jnp
from jax import lax
from jax.experimental import pallas as pl
from jax.experimental.pallas import tpu as pltpu
from jax.sharding import PartitionSpec as P

K = 1536
G = 48
R = 768
BF = jnp.bfloat16
F32 = jnp.float32
MESH = pl.DeviceIdType.MESH

ridge_term = 1.0

CH = 256
NCH = R // CH
LATE = CH // 2
NSEND = NCH + 1
LW = 256
ROWS = 768
KP = 256

NX = 4
NY = 4
RR = 32


def nt(x, y):
    return lax.dot_general(x, y, (((1,), (1,)), ((), ())), preferred_element_type=F32)


def nn(x, y):
    return jnp.dot(x, y, preferred_element_type=F32)


def tn(x, y):
    return lax.dot_general(x, y, (((0,), (0,)), ((), ())), preferred_element_type=F32)


def iota(shape, dim):
    return lax.broadcasted_iota(jnp.int32, shape, dim)


def lane_group(shape):
    lane = iota(shape, 1)
    lane = jnp.where(lane < G, lane, jnp.where(lane < 2 * G, lane - G, lane - 2 * G))
    return jnp.where(iota(shape, 1) < 3 * G, lane, K)


def remote(src, dst, send_sem, recv_sem, device):
    return pltpu.make_async_remote_copy(
        src_ref=src, dst_ref=dst, send_sem=send_sem, recv_sem=recv_sem,
        device_id=(device,), device_id_type=MESH,
    )


def rows_of(c):
    return pl.ds(pl.multiple_of(c * CH, CH), CH)


def late_rows(c):
    return pl.ds(pl.multiple_of(R - CH + c * LATE, LATE), LATE)


def kernel(n, coeff, masks, out, a, s, e, pa, ma, ps, ms, pe, me, mt, mte, far, fart,
           expand, group, rep, mask_in, load_sem, mask_sem,
           rb, to_send, to_recv, on_send, on_recv, leave, eb_send, eb_recv, em_send, em_recv, sb_send, sb_recv, sp_send, sp_recv,
           fe_send, fe_recv, fs_send, fs_recv):
    d = lax.axis_index("pa")
    odd = lax.rem(d, 2)
    sib = d + 1 - 2 * odd
    ext = lax.rem(d + n + 2 * odd - 1, n)
    band_s = (3 - 2 * odd) * R
    band_e = (1 + 2 * odd) * R
    band_far_e = 4 * odd * R
    band_far_s = (4 - 4 * odd) * R
    band_sib_far = 4 * odd * R
    band_ext_far = (4 - 4 * odd) * R

    row = 2 * NX
    plane = row * NY
    place = lax.rem(d, plane)
    base = d - place
    below = lax.rem(base + n - plane, n)
    above = lax.rem(base + plane, n)
    is_last = place == plane - 1
    is_first = place == 0
    is_end = is_last | is_first
    is_up = place == row - 2
    is_down = place == plane - row + 1
    is_relay = is_up | is_down
    relay_out = base + jnp.where(is_last, row - 2, plane - row + 1)
    relay_in = jnp.where(is_last, above + plane - row + 1, below + row - 2)
    relay_from = base + jnp.where(is_up, plane - 1, 0)
    relay_to = jnp.where(is_up, above, below + plane - 1)

    def cols(band, rows):
        return pl.ds(pl.multiple_of(band + rows.start, rows.size), rows.size)

    def whole(band):
        return pl.ds(pl.multiple_of(band, R), R)

    load_mask = pltpu.make_async_copy(masks, mask_in, mask_sem)
    load_mask.start()

    def load(c):
        return pltpu.make_async_copy(coeff.at[rows_of(c), :], a.at[rows_of(c), :], load_sem.at[c])

    def to_ext(rows, c):
        return remote(coeff.at[rows, :], e.at[rows, :], eb_send.at[c], eb_recv.at[c], ext)

    def block_to_ext(c):
        return to_ext(rows_of(c), c)

    late_to_ext = to_ext(late_rows(0), NCH - 1)
    most_to_ext = to_ext(pl.ds(R - LATE, LATE - RR), NCH)
    rest = pl.ds(R - RR, RR)
    rest_to_ext = to_ext(rest, NCH + 1)
    to_relay = remote(coeff.at[rest, :], rb, to_send, to_recv, relay_out)
    from_relay = remote(rb, e.at[rest, :], on_send, on_recv, relay_to)

    def block_to_sib(c):
        return remote(a.at[rows_of(c), :], s.at[rows_of(c), :], sb_send.at[c], sb_recv.at[c], sib)

    def far_to_ext(rows, c):
        return remote(fart.at[rows, :], out.at[rows, whole(band_ext_far)],
                      fe_send.at[c], fe_recv.at[c], ext)

    def far_to_sib(rows, c):
        return remote(far.at[:, cols(0, rows)], out.at[:, cols(band_sib_far, rows)],
                      fs_send.at[c], fs_recv.at[c], sib)

    mask_to_ext = remote(mt, mte, em_send, em_recv, ext)
    m_to_sib = remote(ma, ms, sp_send.at[0], sp_recv.at[0], sib)
    p_to_sib = remote(pa, ps, sp_send.at[1], sp_recv.at[1], sib)

    barrier = pltpu.get_barrier_semaphore()
    pl.semaphore_signal(barrier, inc=1, device_id=(sib,), device_id_type=MESH)
    pl.semaphore_signal(barrier, inc=1, device_id=(ext,), device_id_type=MESH)

    @pl.when(is_relay)
    def _():
        pl.semaphore_signal(barrier, inc=1, device_id=(relay_from,), device_id_type=MESH)
        pl.semaphore_signal(barrier, inc=1, device_id=(relay_to,), device_id_type=MESH)

    pl.loop(0, NCH)(lambda c: load(c).start())
    pl.semaphore_wait(barrier, jnp.where(is_end, 4, 2))

    block_to_ext(0).start()

    @pl.when(is_end)
    def _():
        to_relay.start()
        pl.semaphore_signal(leave, inc=1, device_id=(relay_in,), device_id_type=MESH)


    load_mask.wait()
    mt[...] = mask_in[...].astype(F32).astype(BF)
    mask_to_ext.start()
    pl.loop(1, NCH - 1)(lambda c: block_to_ext(c).start())
    late_to_ext.start()
    most_to_ext.start()

    @pl.when(jnp.logical_not(is_end))
    def _():
        rest_to_ext.start()

    rep[...] = jnp.where(lane_group((G, LW)) == iota((G, LW), 0), 1.0, 0.0).astype(BF)
    ma[...] = tn(mt[...], rep[...]).astype(BF)
    m_to_sib.start()
    for k in range(0, K, KP):
        first = iota((LW, KP), 0) * (K // G)
        column = iota((LW, KP), 1) + k
        expand[:, k:k + KP] = jnp.where(
            (column >= first) & (column < first + K // G), 1.0, 0.0
        ).astype(BF)
        first = lane_group((KP, LW)) * (K // G)
        column = iota((KP, LW), 0) + k
        group[k:k + KP, :] = jnp.where(
            (column >= first) & (column < first + K // G), 1.0, 0.0
        ).astype(BF)

    def split(x):
        first = x.astype(BF)
        rest = x - first.astype(F32)
        second = rest.astype(BF)
        return first, second, (rest - second.astype(F32)).astype(BF)

    def prepare(rows, block, m, p):
        count = rows.size
        m_rows = m[rows, :]
        power = jnp.zeros((count, LW), F32)
        for k in range(0, K, KP):
            keep = nn(m_rows, expand[:, k:k + KP]).astype(BF)
            re = block[rows, k:k + KP] * keep
            im = block[rows, K + k:K + k + KP] * keep
            block[rows, k:k + KP] = re
            block[rows, K + k:K + k + KP] = im
            re = re.astype(F32)
            im = im.astype(F32)
            parts = nn(jnp.concatenate(split(re * re + im * im), axis=0), group[k:k + KP, :])
            power += parts[:count] + parts[count:2 * count] + parts[2 * count:]
        first, second, third = split(power)
        lane = iota((count, LW), 1)
        p[rows, :] = jnp.where(lane < G, first, jnp.where(lane < 2 * G, second, third))

    def score(x, px, mx, left, y, py, my, right):
        numerator = nt(x[left, :], y[right, :])
        norm_left = nt(px[left, :], my[right, :])
        norm_right = nt(mx[left, :], py[right, :])
        return numerator * lax.rsqrt((norm_left + ridge_term) * (norm_right + ridge_term))

    def near(rows, y, py, my, band):
        for i in range(0, R, ROWS):
            left = pl.ds(i, ROWS)
            out[left, cols(band, rows)] = score(a, pa, ma, left, y, py, my, rows).astype(BF)

    @pl.loop(0, NCH)
    def _(c):
        load(c).wait()
        prepare(rows_of(c), a, ma, pa)
        block_to_sib(c).start()

    p_to_sib.start()

    @pl.when(is_relay)
    def _():
        pl.semaphore_wait(leave, 1)
        to_relay.wait_recv()
        from_relay.start()

    @pl.loop(0, NCH)
    def _(c):
        near(rows_of(c), a, pa, ma, 2 * R)

    m_to_sib.wait_recv()
    p_to_sib.wait_recv()

    @pl.loop(0, NCH)
    def _(c):
        block_to_sib(c).wait_recv()
        near(rows_of(c), s, ps, ms, band_s)

    mask_to_ext.wait_recv()
    me[...] = tn(mte[...], rep[...]).astype(BF)

    def with_ext(rows, c):
        prepare(rows, e, me, pe)
        for i in range(0, R, ROWS):
            left = pl.ds(i, ROWS)
            tile = score(s, ps, ms, left, e, pe, me, rows)
            fart[rows, left] = tile.T.astype(BF)
            far[left, cols(0, rows)] = tile.astype(BF)
        far_to_ext(rows, c).start()
        far_to_sib(rows, c).start()
        near(rows, e, pe, me, band_e)

    @pl.loop(0, NCH - 1)
    def _(c):
        block_to_ext(c).wait_recv()
        with_ext(rows_of(c), c)

    @pl.loop(0, 2)
    def _(c):
        @pl.when(c == 0)
        def _():
            late_to_ext.wait_recv()

        @pl.when(c == 1)
        def _():
            most_to_ext.wait_recv()
            pl.when(is_end)(from_relay.wait_recv)
            pl.when(jnp.logical_not(is_end))(rest_to_ext.wait_recv)

        with_ext(late_rows(c), NCH - 1 + c)

    mask_to_ext.wait_send()
    m_to_sib.wait_send()
    p_to_sib.wait_send()
    late_to_ext.wait_send()
    most_to_ext.wait_send()
    pl.when(is_end)(to_relay.wait_send)
    pl.when(jnp.logical_not(is_end))(rest_to_ext.wait_send)
    pl.when(is_relay)(from_relay.wait_send)
    pl.loop(0, NCH - 1)(lambda c: block_to_ext(c).wait_send())
    pl.loop(0, NCH)(lambda c: block_to_sib(c).wait_send())

    @pl.loop(0, NCH - 1)
    def _(c):
        far_to_sib(rows_of(c), c).wait()
        far_to_ext(rows_of(c), c).wait()

    @pl.loop(0, 2)
    def _(c):
        far_to_sib(late_rows(c), NCH - 1 + c).wait()
        far_to_ext(late_rows(c), NCH - 1 + c).wait()


def on_device(coefficients, masks):
    n = lax.axis_size("pa")
    block = pltpu.VMEM((R, 2 * K), BF)
    norm = pltpu.VMEM((R, LW), BF)
    dma = pltpu.SemaphoreType.DMA
    return pl.pallas_call(
        functools.partial(kernel, n),
        out_shape=pltpu.VMEM((R, 5 * R), BF),
        in_specs=[pl.BlockSpec(memory_space=pltpu.HBM)] * 2,
        out_specs=pl.BlockSpec(memory_space=pltpu.VMEM),
        scratch_shapes=[
            block, block, block, norm, norm, norm, norm, norm, norm,
            pltpu.VMEM((G, R), BF), pltpu.VMEM((G, R), BF),
            pltpu.VMEM((R, R), BF), pltpu.VMEM((R, R), BF),
            pltpu.VMEM((LW, K), BF), pltpu.VMEM((K, LW), BF), pltpu.VMEM((G, LW), BF),
            pltpu.VMEM((G, R), jnp.int32),
            dma((NCH,)), dma,
            pltpu.VMEM((RR, 2 * K), BF), dma, dma, dma, dma, pltpu.SemaphoreType.REGULAR,
            dma((NCH + 2,)), dma((NCH + 2,)), dma, dma,
            dma((NCH,)), dma((NCH,)), dma((2,)), dma((2,)),
            dma((NSEND,)), dma((NSEND,)), dma((NSEND,)), dma((NSEND,)),
        ],
        compiler_params=pltpu.CompilerParams(
            collective_id=0, has_side_effects=True, vmem_limit_bytes=56 * 1024 * 1024
        ),
        cost_estimate=pl.CostEstimate(
            flops=2 * 4 * R * R * 2 * K, bytes_accessed=4 * R * 2 * K, transcendentals=4 * R * R
        ),
        name="band",
    )(coefficients, masks.T)


def solution(mesh):
    return jax.shard_map(
        on_device, mesh=mesh, in_specs=(P("pa", None), P("pa", None)),
        out_specs=P("pa", None), check_vma=False,
    )
```

time: 77.5 us -> 75.6 us (0.975)
  Pallas kernels: 74.9 us -> 72.9 us
    pallas_call x1, Pallas kernels: 74.9 us -> 72.9 us  [on_device(): pl.pallas_call(functools.partial(kernel, n), out_shape=pltpu.VMEM((R, 5 *...]
where the time goes in v3:
time: 75.6 us; the launch traced here: 75.5 us
  Pallas kernels  72.9 us (96%)
  local copies, waits for them, and re-layouts  2.58 us (3%)
    pallas_call x1, Pallas kernels, on_device(): pl.pallas_call(functools.partial(kernel, n), out_shape=pltpu.VMEM((R, 5 *...  72.9 us
    unnamed x1, local copies, waits for them, and re-layouts  2.58 us

profile of v3, /device:TPU:0, one launch (start us, length us, event | category | flops | bytes accessed | tf_op | source)
XLA Modules:
  0.0 75.5 jit_solution(7753467739852325013)
XLA Ops:
  0.0 72.9 %band.1 = bf16[768,3840]{1,0:T(8,128)(2,1)S(1)} custom-call(bf16[768,3072]{1,0:T(8,128)(2,1)} %coeff.1, s32[48,768]{1,0:T(8,128)} %bitcast.1), custom_call_target="tpu_custom_call" | custom-call | flops 14495514624 | bytes 9437184 | tf_op jit(solution)/shard_map/band/pallas_call | solution.py:308
  72.9 2.6 %copy.4 = bf16[768,3840]{1,0:T(8,128)(2,1)} copy(bf16[768,3840]{1,0:T(8,128)(2,1)S(1)} %band.1) | data formatting | bytes 11796480

commit v4 on v3

--- a/solution.py
+++ b/solution.py
@@ -26,7 +26,7 @@
 
 NX = 4
 NY = 4
-RR = 32
+RR = 48
 
 
 def nt(x, y):
@@ -68,7 +68,7 @@
 
 def kernel(n, coeff, masks, out, a, s, e, pa, ma, ps, ms, pe, me, mt, mte, far, fart,
            expand, group, rep, mask_in, load_sem, mask_sem,
-           rb, to_send, to_recv, on_send, on_recv, leave, eb_send, eb_recv, em_send, em_recv, sb_send, sb_recv, sp_send, sp_recv,
+           rb, hub_send, hub_recv, spoke_send, spoke_recv, on_send, on_recv, leave, eb_send, eb_recv, em_send, em_recv, sb_send, sb_recv, sp_send, sp_recv,
            fe_send, fe_recv, fs_send, fs_recv):
     d = lax.axis_index("pa")
     odd = lax.rem(d, 2)
@@ -90,13 +90,18 @@
     is_last = place == plane - 1
     is_first = place == 0
     is_end = is_last | is_first
-    is_up = place == row - 2
-    is_down = place == plane - row + 1
-    is_relay = is_up | is_down
-    relay_out = base + jnp.where(is_last, row - 2, plane - row + 1)
-    relay_in = jnp.where(is_last, above + plane - row + 1, below + row - 2)
-    relay_from = base + jnp.where(is_up, plane - 1, 0)
+    level = place // row
+    is_up = (lax.rem(place, row) == row - 2) & (level < 2)
+    is_down = (lax.rem(place, row) == 1) & (level >= NY - 2)
+    level = jnp.where(is_up, level, NY - 1 - level)
+    is_hub = (is_up | is_down) & (level == 0)
+    is_spoke = (is_up | is_down) & (level == 1)
+    step = jnp.where(is_up, row, -row)
+    hub_from = base + jnp.where(is_up, plane - 1, 0)
     relay_to = jnp.where(is_up, above, below + plane - 1)
+    hub_out = base + jnp.where(is_last, row - 2, plane - row + 1)
+    hub_in = jnp.where(is_last, above + plane - row + 1, below + row - 2)
+    spoke_in = hub_in + jnp.where(is_last, -row, row)
 
     def cols(band, rows):
         return pl.ds(pl.multiple_of(band + rows.start, rows.size), rows.size)
@@ -120,8 +125,11 @@
     most_to_ext = to_ext(pl.ds(R - LATE, LATE - RR), NCH)
     rest = pl.ds(R - RR, RR)
     rest_to_ext = to_ext(rest, NCH + 1)
-    to_relay = remote(coeff.at[rest, :], rb, to_send, to_recv, relay_out)
-    from_relay = remote(rb, e.at[rest, :], on_send, on_recv, relay_to)
+    reals, imags = pl.ds(0, K), pl.ds(K, K)
+    to_hub = remote(coeff.at[rest, :], rb, hub_send, hub_recv, hub_out)
+    to_spoke = remote(rb.at[:, imags], rb.at[:, imags], spoke_send, spoke_recv, d + step)
+    from_hub = remote(rb.at[:, reals], e.at[rest, reals], on_send, on_recv.at[0], relay_to)
+    from_spoke = remote(rb.at[:, imags], e.at[rest, imags], on_send, on_recv.at[1], relay_to)
 
     def block_to_sib(c):
         return remote(a.at[rows_of(c), :], s.at[rows_of(c), :], sb_send.at[c], sb_recv.at[c], sib)
@@ -142,21 +150,29 @@
     pl.semaphore_signal(barrier, inc=1, device_id=(sib,), device_id_type=MESH)
     pl.semaphore_signal(barrier, inc=1, device_id=(ext,), device_id_type=MESH)
 
-    @pl.when(is_relay)
-    def _():
-        pl.semaphore_signal(barrier, inc=1, device_id=(relay_from,), device_id_type=MESH)
-        pl.semaphore_signal(barrier, inc=1, device_id=(relay_to,), device_id_type=MESH)
+    def greet(device):
+        pl.semaphore_signal(barrier, inc=1, device_id=(device,), device_id_type=MESH)
+
+    @pl.when(is_hub)
+    def _():
+        greet(hub_from)
+        greet(relay_to)
+
+    @pl.when(is_spoke)
+    def _():
+        greet(d - step)
+        greet(relay_to)
 
     pl.loop(0, NCH)(lambda c: load(c).start())
-    pl.semaphore_wait(barrier, jnp.where(is_end, 4, 2))
+    pl.semaphore_wait(barrier, jnp.where(is_end, 5, jnp.where(is_hub, 3, 2)))
 
     block_to_ext(0).start()
 
     @pl.when(is_end)
     def _():
-        to_relay.start()
-        pl.semaphore_signal(leave, inc=1, device_id=(relay_in,), device_id_type=MESH)
-
+        to_hub.start()
+        for relay in (hub_in, spoke_in):
+            pl.semaphore_signal(leave, inc=1, device_id=(relay,), device_id_type=MESH)
 
     load_mask.wait()
     mt[...] = mask_in[...].astype(F32).astype(BF)
@@ -164,10 +180,7 @@
     pl.loop(1, NCH - 1)(lambda c: block_to_ext(c).start())
     late_to_ext.start()
     most_to_ext.start()
-
-    @pl.when(jnp.logical_not(is_end))
-    def _():
-        rest_to_ext.start()
+    pl.when(jnp.logical_not(is_end))(rest_to_ext.start)
 
     rep[...] = jnp.where(lane_group((G, LW)) == iota((G, LW), 0), 1.0, 0.0).astype(BF)
     ma[...] = tn(mt[...], rep[...]).astype(BF)
@@ -227,11 +240,12 @@
 
     p_to_sib.start()
 
-    @pl.when(is_relay)
-    def _():
+    @pl.when(is_hub)
+    def _():
+        to_hub.wait_recv()
+        to_spoke.start()
         pl.semaphore_wait(leave, 1)
-        to_relay.wait_recv()
-        from_relay.start()
+        from_hub.start()
 
     @pl.loop(0, NCH)
     def _(c):
@@ -245,17 +259,21 @@
         block_to_sib(c).wait_recv()
         near(rows_of(c), s, ps, ms, band_s)
 
+    @pl.when(is_spoke)
+    def _():
+        to_spoke.wait_recv()
+        pl.semaphore_wait(leave, 1)
+        from_spoke.start()
+
     mask_to_ext.wait_recv()
     me[...] = tn(mte[...], rep[...]).astype(BF)
 
     def with_ext(rows, c):
         prepare(rows, e, me, pe)
-        for i in range(0, R, ROWS):
-            left = pl.ds(i, ROWS)
-            tile = score(s, ps, ms, left, e, pe, me, rows)
-            fart[rows, left] = tile.T.astype(BF)
-            far[left, cols(0, rows)] = tile.astype(BF)
+        tile = score(e, pe, me, rows, s, ps, ms, pl.ds(0, R))
+        fart[rows, :] = tile.astype(BF)
         far_to_ext(rows, c).start()
+        far[:, cols(0, rows)] = tile.T.astype(BF)
         far_to_sib(rows, c).start()
         near(rows, e, pe, me, band_e)
 
@@ -273,8 +291,12 @@
         @pl.when(c == 1)
         def _():
             most_to_ext.wait_recv()
-            pl.when(is_end)(from_relay.wait_recv)
             pl.when(jnp.logical_not(is_end))(rest_to_ext.wait_recv)
+
+            @pl.when(is_end)
+            def _():
+                from_hub.wait_recv()
+                from_spoke.wait_recv()
 
         with_ext(late_rows(c), NCH - 1 + c)
 
@@ -283,9 +305,15 @@
     p_to_sib.wait_send()
     late_to_ext.wait_send()
     most_to_ext.wait_send()
-    pl.when(is_end)(to_relay.wait_send)
+    pl.when(is_end)(to_hub.wait_send)
     pl.when(jnp.logical_not(is_end))(rest_to_ext.wait_send)
-    pl.when(is_relay)(from_relay.wait_send)
+    pl.when(is_spoke)(from_spoke.wait_send)
+
+    @pl.when(is_hub)
+    def _():
+        to_spoke.wait_send()
+        from_hub.wait_send()
+
     pl.loop(0, NCH - 1)(lambda c: block_to_ext(c).wait_send())
     pl.loop(0, NCH)(lambda c: block_to_sib(c).wait_send())
 
@@ -317,7 +345,8 @@
             pltpu.VMEM((LW, K), BF), pltpu.VMEM((K, LW), BF), pltpu.VMEM((G, LW), BF),
             pltpu.VMEM((G, R), jnp.int32),
             dma((NCH,)), dma,
-            pltpu.VMEM((RR, 2 * K), BF), dma, dma, dma, dma, pltpu.SemaphoreType.REGULAR,
+            pltpu.VMEM((RR, 2 * K), BF),
+            dma, dma, dma, dma, dma, dma((2,)), pltpu.SemaphoreType.REGULAR,
             dma((NCH + 2,)), dma((NCH + 2,)), dma, dma,
             dma((NCH,)), dma((NCH,)), dma((2,)), dma((2,)),
             dma((NSEND,)), dma((NSEND,)), dma((NSEND,)), dma((NSEND,)),

time: 75.6 us -> 74.3 us (0.983)
  Pallas kernels: 72.9 us -> 71.6 us
    pallas_call x1, Pallas kernels: 72.9 us -> 71.6 us  [on_device(): pl.pallas_call(functools.partial(kernel, n), out_shape=pltpu.VMEM((R, 5 *...]
where the time goes in v4:
time: 74.3 us; the launch traced here: 74.2 us
  Pallas kernels  71.6 us (96%)
  local copies, waits for them, and re-layouts  2.58 us (3%)
    pallas_call x1, Pallas kernels, on_device(): pl.pallas_call(functools.partial(kernel, n), out_shape=pltpu.VMEM((R, 5 *...  71.6 us
    unnamed x1, local copies, waits for them, and re-layouts  2.58 us

profile of v4, /device:TPU:0, one launch (start us, length us, event | category | flops | bytes accessed | tf_op | source)
XLA Modules:
  0.0 74.2 jit_solution(3865402046185431046)
XLA Ops:
  0.0 71.6 %band.1 = bf16[768,3840]{1,0:T(8,128)(2,1)S(1)} custom-call(bf16[768,3072]{1,0:T(8,128)(2,1)} %coeff.1, s32[48,768]{1,0:T(8,128)} %bitcast.1), custom_call_target="tpu_custom_call" | custom-call | flops 14495514624 | bytes 9437184 | tf_op jit(solution)/shard_map/band/pallas_call | solution.py:336
  71.6 2.6 %copy.4 = bf16[768,3840]{1,0:T(8,128)(2,1)} copy(bf16[768,3840]{1,0:T(8,128)(2,1)S(1)} %band.1) | data formatting | bytes 11796480

commit v5 on v4

--- a/solution.py
+++ b/solution.py
@@ -27,6 +27,8 @@
 NX = 4
 NY = 4
 RR = 48
+TR = 32
+TC = 2304
 
 
 def nt(x, y):
@@ -68,7 +70,8 @@
 
 def kernel(n, coeff, masks, out, a, s, e, pa, ma, ps, ms, pe, me, mt, mte, far, fart,
            expand, group, rep, mask_in, load_sem, mask_sem,
-           rb, hub_send, hub_recv, spoke_send, spoke_recv, on_send, on_recv, leave, eb_send, eb_recv, em_send, em_recv, sb_send, sb_recv, sp_send, sp_recv,
+           rb, turn_send, turn_recv, hub_send, hub_recv, spoke_send, spoke_recv,
+           on_send, on_recv, leave, eb_send, eb_recv, em_send, em_recv, sb_send, sb_recv, sp_send, sp_recv,
            fe_send, fe_recv, fs_send, fs_recv):
     d = lax.axis_index("pa")
     odd = lax.rem(d, 2)
@@ -93,6 +96,25 @@
     level = place // row
     is_up = (lax.rem(place, row) == row - 2) & (level < 2)
     is_down = (lax.rem(place, row) == 1) & (level >= NY - 2)
+    column = lax.rem(place, row)
+    is_edge = (column == 0) | (column == row - 1)
+    is_turn_up = column == 3
+    is_turn_down = column == row - 4
+    is_turn = is_turn_up | is_turn_down
+    row_up = base + lax.rem(level + 1, NY) * row
+    row_down = base + lax.rem(level + NY - 1, NY) * row
+    turn_from = jnp.where(is_turn_up, row_down + row - 1, row_up)
+    turn_to = lax.rem(turn_from + n + jnp.where(is_turn_up, 1, -1), n)
+
+    def turn_of(edge):
+        at = lax.rem(edge, plane)
+        level = at // row
+        up = lax.rem(level + 1, NY) * row + 3
+        down = lax.rem(level + NY - 1, NY) * row + row - 4
+        return edge - at + jnp.where(lax.rem(edge, 2) == 1, up, down)
+
+    turn_out = turn_of(d)
+    turn_in = turn_of(ext)
     level = jnp.where(is_up, level, NY - 1 - level)
     is_hub = (is_up | is_down) & (level == 0)
     is_spoke = (is_up | is_down) & (level == 1)
@@ -122,7 +144,19 @@
         return to_ext(rows_of(c), c)
 
     late_to_ext = to_ext(late_rows(0), NCH - 1)
-    most_to_ext = to_ext(pl.ds(R - LATE, LATE - RR), NCH)
+    turned = pl.ds(R - LATE, TR)
+    turned_columns, kept_columns = pl.ds(0, TC), pl.ds(TC, 2 * K - TC)
+
+    def turned_rows_to_ext(columns, c):
+        return remote(coeff.at[turned, columns], e.at[turned, columns],
+                      eb_send.at[c], eb_recv.at[c], ext)
+
+    turned_to_ext = turned_rows_to_ext(turned_columns, NCH + 2)
+    kept_to_ext = turned_rows_to_ext(kept_columns, NCH + 3)
+    most_to_ext = to_ext(pl.ds(R - LATE + TR, LATE - TR - RR), NCH)
+    at_turn = rb.at[0:TR, turned_columns]
+    to_turn = remote(coeff.at[turned, turned_columns], at_turn, turn_send, turn_recv, turn_out)
+    from_turn = remote(at_turn, e.at[turned, turned_columns], on_send, on_recv.at[2], turn_to)
     rest = pl.ds(R - RR, RR)
     rest_to_ext = to_ext(rest, NCH + 1)
     reals, imags = pl.ds(0, K), pl.ds(K, K)
@@ -163,22 +197,38 @@
         greet(d - step)
         greet(relay_to)
 
+    @pl.when(is_turn)
+    def _():
+        greet(turn_from)
+        greet(turn_to)
+
     pl.loop(0, NCH)(lambda c: load(c).start())
-    pl.semaphore_wait(barrier, jnp.where(is_end, 5, jnp.where(is_hub, 3, 2)))
+    greeted = jnp.where(is_end, 5, jnp.where(is_hub, 3, 2)) + jnp.where(is_edge, 2, 0)
+    pl.semaphore_wait(barrier, greeted)
 
     block_to_ext(0).start()
 
+    def allow(device):
+        pl.semaphore_signal(leave, inc=1, device_id=(device,), device_id_type=MESH)
+
+    @pl.when(is_edge)
+    def _():
+        to_turn.start()
+        allow(turn_in)
+
     @pl.when(is_end)
     def _():
         to_hub.start()
-        for relay in (hub_in, spoke_in):
-            pl.semaphore_signal(leave, inc=1, device_id=(relay,), device_id_type=MESH)
+        allow(hub_in)
+        allow(spoke_in)
 
     load_mask.wait()
     mt[...] = mask_in[...].astype(F32).astype(BF)
     mask_to_ext.start()
     pl.loop(1, NCH - 1)(lambda c: block_to_ext(c).start())
     late_to_ext.start()
+    pl.when(jnp.logical_not(is_edge))(turned_to_ext.start)
+    kept_to_ext.start()
     most_to_ext.start()
     pl.when(jnp.logical_not(is_end))(rest_to_ext.start)
 
@@ -240,6 +290,12 @@
 
     p_to_sib.start()
 
+    @pl.when(is_turn)
+    def _():
+        to_turn.wait_recv()
+        pl.semaphore_wait(leave, 1)
+        from_turn.start()
+
     @pl.when(is_hub)
     def _():
         to_hub.wait_recv()
@@ -291,6 +347,9 @@
         @pl.when(c == 1)
         def _():
             most_to_ext.wait_recv()
+            kept_to_ext.wait_recv()
+            pl.when(is_edge)(from_turn.wait_recv)
+            pl.when(jnp.logical_not(is_edge))(turned_to_ext.wait_recv)
             pl.when(jnp.logical_not(is_end))(rest_to_ext.wait_recv)
 
             @pl.when(is_end)
@@ -305,6 +364,10 @@
     p_to_sib.wait_send()
     late_to_ext.wait_send()
     most_to_ext.wait_send()
+    kept_to_ext.wait_send()
+    pl.when(is_edge)(to_turn.wait_send)
+    pl.when(jnp.logical_not(is_edge))(turned_to_ext.wait_send)
+    pl.when(is_turn)(from_turn.wait_send)
     pl.when(is_end)(to_hub.wait_send)
     pl.when(jnp.logical_not(is_end))(rest_to_ext.wait_send)
     pl.when(is_spoke)(from_spoke.wait_send)
@@ -346,8 +409,8 @@
             pltpu.VMEM((G, R), jnp.int32),
             dma((NCH,)), dma,
             pltpu.VMEM((RR, 2 * K), BF),
-            dma, dma, dma, dma, dma, dma((2,)), pltpu.SemaphoreType.REGULAR,
-            dma((NCH + 2,)), dma((NCH + 2,)), dma, dma,
+            dma, dma, dma, dma, dma, dma, dma, dma((3,)), pltpu.SemaphoreType.REGULAR,
+            dma((NCH + 4,)), dma((NCH + 4,)), dma, dma,
             dma((NCH,)), dma((NCH,)), dma((2,)), dma((2,)),
             dma((NSEND,)), dma((NSEND,)), dma((NSEND,)), dma((NSEND,)),
         ],

time: 74.3 us -> 73.3 us (0.987)
  Pallas kernels: 71.6 us -> 70.2 us
    pallas_call x1, Pallas kernels: 71.6 us -> 70.2 us  [on_device(): pl.pallas_call(functools.partial(kernel, n), out_shape=pltpu.VMEM((R, 5 *...]
where the time goes in v5:
time: 73.3 us; the launch traced here: 72.8 us
  Pallas kernels  70.2 us (96%)
  local copies, waits for them, and re-layouts  2.58 us (4%)
    pallas_call x1, Pallas kernels, on_device(): pl.pallas_call(functools.partial(kernel, n), out_shape=pltpu.VMEM((R, 5 *...  70.2 us
    unnamed x1, local copies, waits for them, and re-layouts  2.58 us

profile of v5, /device:TPU:0, one launch (start us, length us, event | category | flops | bytes accessed | tf_op | source)
XLA Modules:
  0.0 72.8 jit_solution(9298590390567368465)
XLA Ops:
  0.0 70.2 %band.1 = bf16[768,3840]{1,0:T(8,128)(2,1)S(1)} custom-call(bf16[768,3072]{1,0:T(8,128)(2,1)} %coeff.1, s32[48,768]{1,0:T(8,128)} %bitcast.1), custom_call_target="tpu_custom_call" | custom-call | flops 14495514624 | bytes 9437184 | tf_op jit(solution)/shard_map/band/pallas_call | solution.py:399
  70.2 2.6 %copy.4 = bf16[768,3840]{1,0:T(8,128)(2,1)} copy(bf16[768,3840]{1,0:T(8,128)(2,1)S(1)} %band.1) | data formatting | bytes 11796480

commit v6 on v5

--- a/solution.py
+++ b/solution.py
@@ -28,7 +28,7 @@
 NY = 4
 RR = 48
 TR = 32
-TC = 2304
+TC = 2048
 
 
 def nt(x, y):
@@ -71,7 +71,7 @@
 def kernel(n, coeff, masks, out, a, s, e, pa, ma, ps, ms, pe, me, mt, mte, far, fart,
            expand, group, rep, mask_in, load_sem, mask_sem,
            rb, turn_send, turn_recv, hub_send, hub_recv, spoke_send, spoke_recv,
-           on_send, on_recv, leave, eb_send, eb_recv, em_send, em_recv, sb_send, sb_recv, sp_send, sp_recv,
+           on_send, on_recv, leave, vouch, eb_send, eb_recv, em_send, em_recv, sb_send, sb_recv, sp_send, sp_recv,
            fe_send, fe_recv, fs_send, fs_recv):
     d = lax.axis_index("pa")
     odd = lax.rem(d, 2)
@@ -190,21 +190,17 @@
     @pl.when(is_hub)
     def _():
         greet(hub_from)
+
+    @pl.when(is_hub | is_spoke)
+    def _():
         greet(relay_to)
 
-    @pl.when(is_spoke)
-    def _():
-        greet(d - step)
-        greet(relay_to)
-
     @pl.when(is_turn)
     def _():
-        greet(turn_from)
         greet(turn_to)
 
     pl.loop(0, NCH)(lambda c: load(c).start())
-    greeted = jnp.where(is_end, 5, jnp.where(is_hub, 3, 2)) + jnp.where(is_edge, 2, 0)
-    pl.semaphore_wait(barrier, greeted)
+    pl.semaphore_wait(barrier, jnp.where(is_end, 6, jnp.where(is_edge, 3, 2)))
 
     block_to_ext(0).start()
 
@@ -213,8 +209,8 @@
 
     @pl.when(is_edge)
     def _():
-        to_turn.start()
         allow(turn_in)
+        pl.semaphore_signal(vouch, inc=1, device_id=(ext,), device_id_type=MESH)
 
     @pl.when(is_end)
     def _():
@@ -282,6 +278,11 @@
             left = pl.ds(i, ROWS)
             out[left, cols(band, rows)] = score(a, pa, ma, left, y, py, my, rows).astype(BF)
 
+    @pl.when(is_edge)
+    def _():
+        pl.semaphore_wait(vouch, 1)
+        to_turn.start()
+
     @pl.loop(0, NCH)
     def _(c):
         load(c).wait()
@@ -299,8 +300,8 @@
     @pl.when(is_hub)
     def _():
         to_hub.wait_recv()
+        pl.semaphore_wait(leave, 1)
         to_spoke.start()
-        pl.semaphore_wait(leave, 1)
         from_hub.start()
 
     @pl.loop(0, NCH)
@@ -328,7 +329,11 @@
         prepare(rows, e, me, pe)
         tile = score(e, pe, me, rows, s, ps, ms, pl.ds(0, R))
         fart[rows, :] = tile.astype(BF)
-        far_to_ext(rows, c).start()
+
+        @pl.when(c == NCH)
+        def _():
+            far_to_ext(rows, c).start()
+
         far[:, cols(0, rows)] = tile.T.astype(BF)
         far_to_sib(rows, c).start()
         near(rows, e, pe, me, band_e)
@@ -336,6 +341,7 @@
     @pl.loop(0, NCH - 1)
     def _(c):
         block_to_ext(c).wait_recv()
+        pl.when(c > 0)(lambda: far_to_ext(rows_of(c - 1), c - 1).start())
         with_ext(rows_of(c), c)
 
     @pl.loop(0, 2)
@@ -343,6 +349,7 @@
         @pl.when(c == 0)
         def _():
             late_to_ext.wait_recv()
+            far_to_ext(rows_of(NCH - 2), NCH - 2).start()
 
         @pl.when(c == 1)
         def _():
@@ -356,6 +363,8 @@
             def _():
                 from_hub.wait_recv()
                 from_spoke.wait_recv()
+
+            far_to_ext(late_rows(0), NCH - 1).start()
 
         with_ext(late_rows(c), NCH - 1 + c)
 
@@ -409,7 +418,8 @@
             pltpu.VMEM((G, R), jnp.int32),
             dma((NCH,)), dma,
             pltpu.VMEM((RR, 2 * K), BF),
-            dma, dma, dma, dma, dma, dma, dma, dma((3,)), pltpu.SemaphoreType.REGULAR,
+            dma, dma, dma, dma, dma, dma, dma, dma((3,)),
+            pltpu.SemaphoreType.REGULAR, pltpu.SemaphoreType.REGULAR,
             dma((NCH + 4,)), dma((NCH + 4,)), dma, dma,
             dma((NCH,)), dma((NCH,)), dma((2,)), dma((2,)),
             dma((NSEND,)), dma((NSEND,)), dma((NSEND,)), dma((NSEND,)),

time: 73.3 us -> 73 us (level)
  no operation moved by 1% of the time
where the time goes in v6:
time: 73 us; the launch traced here: 72.9 us
  Pallas kernels  70.3 us (96%)
  local copies, waits for them, and re-layouts  2.58 us (4%)
    pallas_call x1, Pallas kernels, on_device(): pl.pallas_call(functools.partial(kernel, n), out_shape=pltpu.VMEM((R, 5 *...  70.3 us
    unnamed x1, local copies, waits for them, and re-layouts  2.58 us

profile of v6, /device:TPU:0, one launch (start us, length us, event | category | flops | bytes accessed | tf_op | source)
XLA Modules:
  0.0 72.9 jit_solution(12383850917523680620)
XLA Ops:
  0.0 70.3 %band.1 = bf16[768,3840]{1,0:T(8,128)(2,1)S(1)} custom-call(bf16[768,3072]{1,0:T(8,128)(2,1)} %coeff.1, s32[48,768]{1,0:T(8,128)} %bitcast.1), custom_call_target="tpu_custom_call" | custom-call | flops 14495514624 | bytes 9437184 | tf_op jit(solution)/shard_map/band/pallas_call | solution.py:408
  70.3 2.6 %copy.4 = bf16[768,3840]{1,0:T(8,128)(2,1)} copy(bf16[768,3840]{1,0:T(8,128)(2,1)S(1)} %band.1) | data formatting | bytes 11796480

commit v7 on v6

--- a/solution.py
+++ b/solution.py
@@ -28,7 +28,8 @@
 NY = 4
 RR = 48
 TR = 32
-TC = 2048
+TC = 2304
+TE = 1920
 
 
 def nt(x, y):
@@ -70,7 +71,8 @@
 
 def kernel(n, coeff, masks, out, a, s, e, pa, ma, ps, ms, pe, me, mt, mte, far, fart,
            expand, group, rep, mask_in, load_sem, mask_sem,
-           rb, turn_send, turn_recv, hub_send, hub_recv, spoke_send, spoke_recv,
+           rb, turn_send, turn_recv, mid_send, mid_recv, mid_on_send, mid_on_recv,
+           hub_send, hub_recv, spoke_send, spoke_recv,
            on_send, on_recv, leave, vouch, eb_send, eb_recv, em_send, em_recv, sb_send, sb_recv, sp_send, sp_recv,
            fe_send, fe_recv, fs_send, fs_recv):
     d = lax.axis_index("pa")
@@ -101,6 +103,9 @@
     is_turn_up = column == 3
     is_turn_down = column == row - 4
     is_turn = is_turn_up | is_turn_down
+    turns_end = jnp.where(is_turn_up, level == 0, level == NY - 1)
+    turns_mid = is_turn & jnp.logical_not(turns_end)
+    is_mid = is_edge & jnp.logical_not(is_end)
     row_up = base + lax.rem(level + 1, NY) * row
     row_down = base + lax.rem(level + NY - 1, NY) * row
     turn_from = jnp.where(is_turn_up, row_down + row - 1, row_up)
@@ -132,7 +137,6 @@
         return pl.ds(pl.multiple_of(band, R), R)
 
     load_mask = pltpu.make_async_copy(masks, mask_in, mask_sem)
-    load_mask.start()
 
     def load(c):
         return pltpu.make_async_copy(coeff.at[rows_of(c), :], a.at[rows_of(c), :], load_sem.at[c])
@@ -145,7 +149,8 @@
 
     late_to_ext = to_ext(late_rows(0), NCH - 1)
     turned = pl.ds(R - LATE, TR)
-    turned_columns, kept_columns = pl.ds(0, TC), pl.ds(TC, 2 * K - TC)
+    turned_columns, mid_columns = pl.ds(0, TE), pl.ds(TE, TC - TE)
+    kept_columns = pl.ds(TC, 2 * K - TC)
 
     def turned_rows_to_ext(columns, c):
         return remote(coeff.at[turned, columns], e.at[turned, columns],
@@ -154,6 +159,11 @@
     turned_to_ext = turned_rows_to_ext(turned_columns, NCH + 2)
     kept_to_ext = turned_rows_to_ext(kept_columns, NCH + 3)
     most_to_ext = to_ext(pl.ds(R - LATE + TR, LATE - TR - RR), NCH)
+    mid_to_ext = turned_rows_to_ext(mid_columns, NCH + 4)
+    mid_at_turn = rb.at[0:TR, mid_columns]
+    mid_to_turn = remote(coeff.at[turned, mid_columns], mid_at_turn, mid_send, mid_recv, turn_out)
+    mid_from_turn = remote(mid_at_turn, e.at[turned, mid_columns], mid_on_send, mid_on_recv,
+                           turn_to)
     at_turn = rb.at[0:TR, turned_columns]
     to_turn = remote(coeff.at[turned, turned_columns], at_turn, turn_send, turn_recv, turn_out)
     from_turn = remote(at_turn, e.at[turned, turned_columns], on_send, on_recv.at[2], turn_to)
@@ -181,8 +191,8 @@
     p_to_sib = remote(pa, ps, sp_send.at[1], sp_recv.at[1], sib)
 
     barrier = pltpu.get_barrier_semaphore()
+    pl.semaphore_signal(barrier, inc=1, device_id=(ext,), device_id_type=MESH)
     pl.semaphore_signal(barrier, inc=1, device_id=(sib,), device_id_type=MESH)
-    pl.semaphore_signal(barrier, inc=1, device_id=(ext,), device_id_type=MESH)
 
     def greet(device):
         pl.semaphore_signal(barrier, inc=1, device_id=(device,), device_id_type=MESH)
@@ -199,6 +209,7 @@
     def _():
         greet(turn_to)
 
+    load_mask.start()
     pl.loop(0, NCH)(lambda c: load(c).start())
     pl.semaphore_wait(barrier, jnp.where(is_end, 6, jnp.where(is_edge, 3, 2)))
 
@@ -224,6 +235,7 @@
     pl.loop(1, NCH - 1)(lambda c: block_to_ext(c).start())
     late_to_ext.start()
     pl.when(jnp.logical_not(is_edge))(turned_to_ext.start)
+    pl.when(jnp.logical_not(is_mid))(mid_to_ext.start)
     kept_to_ext.start()
     most_to_ext.start()
     pl.when(jnp.logical_not(is_end))(rest_to_ext.start)
@@ -282,6 +294,7 @@
     def _():
         pl.semaphore_wait(vouch, 1)
         to_turn.start()
+        pl.when(is_mid)(mid_to_turn.start)
 
     @pl.loop(0, NCH)
     def _(c):
@@ -296,6 +309,11 @@
         to_turn.wait_recv()
         pl.semaphore_wait(leave, 1)
         from_turn.start()
+
+        @pl.when(turns_mid)
+        def _():
+            mid_to_turn.wait_recv()
+            mid_from_turn.start()
 
     @pl.when(is_hub)
     def _():
@@ -355,6 +373,8 @@
         def _():
             most_to_ext.wait_recv()
             kept_to_ext.wait_recv()
+            pl.when(is_mid)(mid_from_turn.wait_recv)
+            pl.when(jnp.logical_not(is_mid))(mid_to_ext.wait_recv)
             pl.when(is_edge)(from_turn.wait_recv)
             pl.when(jnp.logical_not(is_edge))(turned_to_ext.wait_recv)
             pl.when(jnp.logical_not(is_end))(rest_to_ext.wait_recv)
@@ -374,6 +394,9 @@
     late_to_ext.wait_send()
     most_to_ext.wait_send()
     kept_to_ext.wait_send()
+    pl.when(is_mid)(mid_to_turn.wait_send)
+    pl.when(jnp.logical_not(is_mid))(mid_to_ext.wait_send)
+    pl.when(turns_mid)(mid_from_turn.wait_send)
     pl.when(is_edge)(to_turn.wait_send)
     pl.when(jnp.logical_not(is_edge))(turned_to_ext.wait_send)
     pl.when(is_turn)(from_turn.wait_send)
@@ -418,9 +441,10 @@
             pltpu.VMEM((G, R), jnp.int32),
             dma((NCH,)), dma,
             pltpu.VMEM((RR, 2 * K), BF),
-            dma, dma, dma, dma, dma, dma, dma, dma((3,)),
+            dma, dma, dma, dma, dma, dma,
+            dma, dma, dma, dma, dma, dma((3,)),
             pltpu.SemaphoreType.REGULAR, pltpu.SemaphoreType.REGULAR,
-            dma((NCH + 4,)), dma((NCH + 4,)), dma, dma,
+            dma((NCH + 5,)), dma((NCH + 5,)), dma, dma,
             dma((NCH,)), dma((NCH,)), dma((2,)), dma((2,)),
             dma((NSEND,)), dma((NSEND,)), dma((NSEND,)), dma((NSEND,)),
         ],

time: 73 us -> 73.1 us (level)
  no operation moved by 1% of the time
where the time goes in v7:
time: 73.1 us; the launch traced here: 73 us
  Pallas kernels  70.4 us (96%)
  local copies, waits for them, and re-layouts  2.58 us (4%)
    pallas_call x1, Pallas kernels, on_device(): pl.pallas_call(functools.partial(kernel, n), out_shape=pltpu.VMEM((R, 5 *...  70.4 us
    unnamed x1, local copies, waits for them, and re-layouts  2.58 us

profile of v7, /device:TPU:0, one launch (start us, length us, event | category | flops | bytes accessed | tf_op | source)
XLA Modules:
  0.0 73.0 jit_solution(3421122201907909836)
XLA Ops:
  0.0 70.4 %band.1 = bf16[768,3840]{1,0:T(8,128)(2,1)S(1)} custom-call(bf16[768,3072]{1,0:T(8,128)(2,1)} %coeff.1, s32[48,768]{1,0:T(8,128)} %bitcast.1), custom_call_target="tpu_custom_call" | custom-call | flops 14495514624 | bytes 9437184 | tf_op jit(solution)/shard_map/band/pallas_call | solution.py:431
  70.4 2.6 %copy.4 = bf16[768,3840]{1,0:T(8,128)(2,1)} copy(bf16[768,3840]{1,0:T(8,128)(2,1)S(1)} %band.1) | data formatting | bytes 11796480

commit v8 on v7

--- a/solution.py
+++ b/solution.py
@@ -29,7 +29,7 @@
 RR = 48
 TR = 32
 TC = 2304
-TE = 1920
+TE = 1664
 
 
 def nt(x, y):

time: 73.1 us -> 73.2 us (level)
  no operation moved by 1% of the time
where the time goes in v8:
time: 73.2 us
  Pallas kernels  70.6 us (96%)
  local copies, waits for them, and re-layouts  2.58 us (4%)
    pallas_call x1, Pallas kernels, on_device(): pl.pallas_call(functools.partial(kernel, n), out_shape=pltpu.VMEM((R, 5 *...  70.6 us
    unnamed x1, local copies, waits for them, and re-layouts  2.58 us

profile of v8, /device:TPU:0, one launch (start us, length us, event | category | flops | bytes accessed | tf_op | source)
XLA Modules:
  0.0 73.2 jit_solution(5823392340633025245)
XLA Ops:
  0.0 70.6 %band.1 = bf16[768,3840]{1,0:T(8,128)(2,1)S(1)} custom-call(bf16[768,3072]{1,0:T(8,128)(2,1)} %coeff.1, s32[48,768]{1,0:T(8,128)} %bitcast.1), custom_call_target="tpu_custom_call" | custom-call | flops 14495514624 | bytes 9437184 | tf_op jit(solution)/shard_map/band/pallas_call | solution.py:431
  70.6 2.6 %copy.4 = bf16[768,3840]{1,0:T(8,128)(2,1)} copy(bf16[768,3840]{1,0:T(8,128)(2,1)S(1)} %band.1) | data formatting | bytes 11796480
